TPU v7x, 512 devices: a whole 4x8x8 slice. The times are simulated.
512 devices in a mesh: seq: 128 (over y, z, core), win: 4 (over x).
Axes of the slice: x: 4, y: 8, z: 8, core: 2. Of those that a mesh axis runs over, the one named last changes fastest.
Arguments:
- queries: bfloat16 [65536, 1024], P(('win', 'seq')), parts along dimension 0, may hold values from -6 to 6
- key_rows: bfloat16 [65536, 1024], P(('win', 'seq')), parts along dimension 0, may hold values from -6 to 6
- value_rows: bfloat16 [65536, 2048], P(('win', 'seq')), parts along dimension 0, may hold values from -6 to 6
- residual: bfloat16 [65536, 1024], P(('win', 'seq')), parts along dimension 0, may hold values from -6 to 6
- out_weight: bfloat16 [2048, 1024], P(None, 'seq'), may hold values from -0.125 to 0.125
- expert_in: bfloat16 [128, 1024, 768], P('seq'), may hold values from -0.1875 to 0.1875
- expert_out: bfloat16 [128, 384, 1024], P('seq'), may hold values from -0.3125 to 0.3125
- expert_ids: int32 [65536, 2], P(('win', 'seq')), parts along dimension 0, may hold values from 0 to 127, all different within a row; in each aligned block of 128 rows (0 to 127, 128 to 255, ...) at most 4 rows name the same one
- gate_values: float32 [65536, 2], P(('win', 'seq')), parts along dimension 0, may hold values from 0.2 to 1
Outputs:
- layer_out: bfloat16 [65536, 1024], P(('win', 'seq')), parts along dimension 0
There are 4 independent parts, one for each index of `win`. A program takes and returns all parts, laid end to end along the dimension named above; an argument that names none is the same for every part. Nothing has to cross between parts.
Inputs may be any that keep to these rules, and one draw needn't show every extreme that they name: `expert_ids`: the 2 ids of a row differ. Within the rows of one block of 128 tokens no expert is named by more than 4 rows, a bound that some block reaches. Every expert is named somewhere.
All inputs are finite; a program needn't handle non-finite values.
Results may differ from a plain program's by a relative error of at most 0.013.
Values may be sent and summed in bfloat16 or wider, within the bound.
A program may use at most 128 MiB of HBM per device.

v0:
```python
import jax
import jax.numpy as jnp
from jax import lax
from jax.sharding import PartitionSpec as P

D = 1024
H = 16
DK = 64
DV = 128
HE = 384
TOP = 2


def carried_in(x, axis, join, neutral):
    place = lax.axis_index(axis)
    gathered = lax.all_gather(x.astype(jnp.bfloat16), axis)
    state = jnp.zeros_like(x) + jnp.asarray(neutral, x.dtype)

    def one(step, state):
        return join(state, lax.dynamic_index_in_dim(gathered, step, 0, False).astype(x.dtype))

    return lax.fori_loop(0, place, one, state)


def add_states(earlier, later):
    return earlier + later


def per_device(
    queries,
    key_rows,
    value_rows,
    residual,
    out_weight,
    expert_in,
    expert_out,
    expert_ids,
    gate_values,
):
    length = queries.shape[0]
    q_heads = queries.reshape(length, H, DK)
    k_heads = key_rows.reshape(length, H, DK)
    v_heads = value_rows.reshape(length, H, DV)
    local_state = jnp.einsum("thd,the->hde", k_heads, v_heads, preferred_element_type=jnp.float32)
    prefix = carried_in(local_state, "seq", add_states, jnp.zeros_like(local_state))
    causal = jnp.arange(length)[:, None] >= jnp.arange(length)[None, :]
    scores = jnp.einsum("thd,shd->hts", q_heads, k_heads, preferred_element_type=jnp.float32)
    scores = jnp.where(causal[None], scores, 0.0).astype(jnp.bfloat16)
    intra_sum = jnp.einsum("hts,she->the", scores, v_heads, preferred_element_type=jnp.float32)
    inter_sum = jnp.einsum(
        "thd,hde->the", q_heads.astype(jnp.float32), prefix, precision=lax.Precision.HIGHEST
    )
    position = (lax.axis_index("seq") * length + jnp.arange(length)).astype(jnp.float32)
    scaling = lax.rsqrt((position + 1.0) * DK)
    attended = (
        ((intra_sum + inter_sum) * scaling[:, None, None])
        .astype(jnp.bfloat16)
        .reshape(length, H * DV)
    )
    projected = jnp.dot(
        attended,
        lax.all_gather(out_weight, "seq", axis=1, tiled=True),
        preferred_element_type=jnp.float32,
    )
    hidden = (residual.astype(jnp.float32) + projected).astype(jnp.bfloat16)
    hidden_float = hidden.astype(jnp.float32)
    normed = (
        hidden_float
        * lax.rsqrt(jnp.mean(hidden_float * hidden_float, axis=-1, keepdims=True) + 1e-06)
    ).astype(jnp.bfloat16)
    experts = lax.axis_size("seq") * expert_in.shape[0]
    capacity = max(2, 2 * length * TOP // experts)
    flat_ids = expert_ids.reshape(-1)
    one_hot = (flat_ids[:, None] == jnp.arange(experts)[None, :]).astype(jnp.int32)
    earlier = jnp.cumsum(one_hot, axis=0) - one_hot
    slot_index = jnp.sum(earlier * one_hot, axis=-1)
    dest_row = flat_ids * capacity + slot_index
    buffer = (
        jnp.zeros((experts * capacity, D), jnp.bfloat16)
        .at[dest_row]
        .set(jnp.repeat(normed, TOP, axis=0))
    )
    buffer = buffer.reshape(experts, 1, capacity, D)
    act = jnp.einsum(
        "ensd,edf->ensf",
        lax.all_to_all(buffer, "seq", split_axis=0, concat_axis=1, tiled=True),
        expert_in,
        preferred_element_type=jnp.float32,
    )
    inner = (jax.nn.silu(act[..., :HE]) * act[..., HE:]).astype(jnp.bfloat16)
    produced_all = jnp.einsum(
        "ensf,efd->ensd", inner, expert_out, preferred_element_type=jnp.float32
    ).astype(jnp.bfloat16)
    returned_rows = lax.all_to_all(produced_all, "seq", split_axis=1, concat_axis=0, tiled=True)
    picked = returned_rows.reshape(experts * capacity, D)[dest_row]
    combined = jnp.sum(
        picked.astype(jnp.float32).reshape(length, TOP, D) * gate_values[:, :, None], axis=1
    )
    return (hidden_float + combined).astype(jnp.bfloat16)


def solution(mesh):
    in_specs = (
        P(("win", "seq"), None),
        P(("win", "seq"), None),
        P(("win", "seq"), None),
        P(("win", "seq"), None),
        P(None, "seq"),
        P("seq", None, None),
        P("seq", None, None),
        P(("win", "seq"), None),
        P(("win", "seq"), None),
    )
    out_specs = P(("win", "seq"), None)
    return jax.shard_map(
        per_device, mesh=mesh, in_specs=in_specs, out_specs=out_specs, check_vma=False
    )
```

profile of v0, /device:TPU:2, one launch (start us, length us, event | category | flops | bytes accessed | tf_op | source)
XLA Modules:
  0.0 401.8 jit_solution(2190676096343332066)
XLA Ops:
  6.5 1.2 copy.28
  7.8 2.0 convolution_convert_fusion.1
  9.9 0.7 all-gather.4.cloned.1.call-update
  11.3 0.2 fusion.26
  12.1 1.7 convolution_bitcast_fusion.1
  13.9 142.8 %all-gather.6.cloned.1.call-done = bf16[2048,64,128]{2,1,0:T(8,128)(2,1)} async-done(((bf16[16,64,128]{2,1,0:T(8,128)(2,1)}), bf16[2048,64,128]{2,1,0:T(8,128)(2,1)}) %all-gather.6.cloned.1.call-update) | async-done | bytes 33554448 | tf_op jit(solution)/shard_map/all_gather | solution.py:16
  156.8 1.8 fusion.8
  158.6 83.9 %all-gather.4.cloned.1.call-done = bf16[2048,1024]{0,1:T(8,128)(2,1)} async-done(((bf16[2048,8]{0,1:T(8,128)(2,1)}), bf16[2048,1024]{0,1:T(8,128)(2,1)}) %all-gather.4.cloned.1.call-update) | async-done | bytes 4194320 | tf_op jit(solution)/shard_map/all_gather | solution.py:62
  242.4 4.0 multiply_reduce_fusion.1
  246.5 0.3 broadcast_in_dim.34
  246.8 1.0 reshape.151
  247.8 2.4 scatter_custom_fusion
  250.2 1.2 reshape.131
  251.4 94.1 %all_to_all.8 = bf16[128,1,4,1024]{3,2,1,0:T(4,128)(2,1)S(1)} all-to-all(bf16[128,1,4,1024]{3,2,1,0:T(4,128)(2,1)} %bitcast.76), channel_id=1, replica_groups=mesh['seq'=128,'win'=4] {'seq'}, dimensions={0} | all-to-all | bytes 2097152 | tf_op jit(solution)/shard_map/all_to_all | solution.py:86
  345.5 1.4 fusion.2
  346.9 0.7 fusion.5
  347.6 1.8 copy.38
  349.5 7.6 %all-to-all-start.1 = ((bf16[1,128,4,1024]{3,2,0,1:T(4,128)(2,1)}), bf16[1,128,4,1024]{3,2,0,1:T(4,128)(2,1)}, u32[]{:S(2)}, u32[]{:S(2)}) async-start(bf16[1,128,4,1024]{3,2,0,1:T(4,128)(2,1)} %copy.38), calls=%async_computation.1 | async-start | bytes 2097152 | tf_op jit(solution)/shard_map/all_to_all | solution.py:94
  357.3 30.5 %all-to-all-done.1 = bf16[1,128,4,1024]{3,2,0,1:T(4,128)(2,1)} async-done(((bf16[1,128,4,1024]{3,2,0,1:T(4,128)(2,1)}), bf16[1,128,4,1024]{3,2,0,1:T(4,128)(2,1)}, u32[]{:S(2)}, u32[]{:S(2)}) %all-to-all-start.1) | async-done | bytes 1048608 | tf_op jit(solution)/shard_map/all_to_all | solution.py:94
  387.8 1.3 reshape.136
  389.1 2.0 gather_fusion
  391.1 1.7 reshape.138
  392.8 1.3 multiply_reduce_fusion
  394.1 0.8 add_convert_fusion
  (37 shorter events, 1.6 us)
Async XLA Ops:
  6.5 339.0 %copy-start = (bf16[1,1024,768]{2,1,0:T(8,128)(2,1)S(1)}, bf16[1,1024,768]{2,1,0:T(8,128)(2,1)}, u32[]{:S(2)}) copy-start(bf16[1,1024,768]{2,1,0:T(8,128)(2,1)} %param.16) | copy-start | bytes 4718596
  6.5 4.1 %copy-start.2 = (s32[128,2]{0,1:T(2,128)S(1)}, s32[128,2]{0,1:T(2,128)}, u32[]{:S(2)}) copy-start(s32[128,2]{0,1:T(2,128)} %param.18) | copy-start | bytes 3076
  6.5 4.5 %copy-start.1 = (bf16[128,1024]{1,0:T(8,128)(2,1)S(1)}, bf16[128,1024]{1,0:T(8,128)(2,1)}, u32[]{:S(2)}) copy-start(bf16[128,1024]{1,0:T(8,128)(2,1)} %param.11) | copy-start | bytes 786436
  6.5 150.1 %all-gather.6.cloned.1.call-start = ((), (), s32[]{:S(2)}) async-start(), calls=%async_computation.3 | async-start | bytes 33816576 | tf_op jit(solution)/shard_map/all_gather | solution.py:16
  9.8 232.6 %all-gather.4.cloned.1.call-start = ((), (), s32[]{:S(2)}) async-start(), calls=%async_computation.2 | async-start | bytes 4227072 | tf_op jit(solution)/shard_map/all_gather | solution.py:62
  345.5 1.4 copy-start.4
  349.5 7.6 %copy-start.3 = (f32[128,2]{0,1:T(2,128)S(1)}, f32[128,2]{0,1:T(2,128)}, u32[]{:S(2)}) copy-start(f32[128,2]{0,1:T(2,128)} %param.19) | copy-start | bytes 3076
  349.5 38.3 %all-to-all-start.1 = ((bf16[1,128,4,1024]{3,2,0,1:T(4,128)(2,1)}), bf16[1,128,4,1024]{3,2,0,1:T(4,128)(2,1)}, u32[]{:S(2)}, u32[]{:S(2)}) async-start(bf16[1,128,4,1024]{3,2,0,1:T(4,128)(2,1)} %copy.38), calls=%async_computation.1 | async-start | bytes 2097152 | tf_op jit(solution)/shard_map/all_to_all | solution.py:94
Sparse Core Ops, SparseCore 0:
  10.5 146.1 all-gather.5
  159.8 82.5 all-gather.3
where the time goes:
time: 406 us; the launch traced here: 402 us
  waiting for transfers between devices  258 us (64%)
  blocking collectives  94.1 us (23%)
  local copies, waits for them, and re-layouts  14.1 us (3%)
  between operations  13.6 us (3%)
  matrix products  11.6 us (3%)
  starting transfers between devices  7.67 us (2%)
    all_gather x1, waiting for transfers between devices, carried_in(): gathered = lax.all_gather(x.astype(jnp.bfloat16), axis)  143 us
    all_to_all x1, blocking collectives, per_device(): lax.all_to_all(buffer, 'seq', split_axis=0, concat_axis=1, tiled=True)  94.1 us
    all_gather x1, waiting for transfers between devices, per_device(): lax.all_gather(out_weight, 'seq', axis=1, tiled=True)  83.9 us
    all_to_all x1, waiting for transfers between devices, per_device(): lax.all_to_all(produced_all, 'seq', split_axis=1, concat_axis=0, tiled=True)  30.5 us
  transfers between devices with their start and end apart: 3, of which 3 were waited for; matrix products, arithmetic and copies ran while one was open for 1% of the time, Pallas kernels for 0%

commit v1 on v0

--- a/solution.py
+++ b/solution.py
@@ -59,7 +59,9 @@
     )
     projected = jnp.dot(
         attended,
-        lax.all_gather(out_weight, "seq", axis=1, tiled=True),
+        jnp.concatenate(
+            lax.all_to_all(jnp.stack([out_weight] * lax.axis_size("seq")), "seq", 0, 0), axis=1
+        ),
         preferred_element_type=jnp.float32,
     )
     hidden = (residual.astype(jnp.float32) + projected).astype(jnp.bfloat16)

time: 406 us -> 491 us (1.21)
  blocking collectives: 94.1 us -> 177 us
  waiting for transfers between devices: 258 us -> 238 us
  starting transfers between devices: 7.67 us -> 25.8 us
    all_gather x1 -> x0, waiting for transfers between devices: 83.9 us -> none  [per_device(): lax.all_gather(out_weight, 'seq', axis=1, tiled=True)]
    all_to_all x1, blocking collectives: 94.1 us -> 177 us  [per_device(): lax.all_to_all(buffer, 'seq', split_axis=0, concat_axis=1, tiled=True)]
    all_gather x1, waiting for transfers between devices: 143 us -> 208 us  [carried_in(): gathered = lax.all_gather(x.astype(jnp.bfloat16), axis)]
    all_to_all x0 -> x1, starting transfers between devices: none -> 18.5 us  [per_device(): lax.all_to_all(jnp.stack([out_weight] * lax.axis_size('seq')), 'seq', 0, 0)]
  transfers between devices with their start and end apart: 3 -> 3, of which waited for: 3 -> 2; matrix products, arithmetic and copies ran while one was open for 1% -> 2% of each run, Pallas kernels for 0% -> 0%
where the time goes in v1:
time: 491 us; the launch traced here: 487 us
  waiting for transfers between devices  238 us (48%)
  blocking collectives  177 us (36%)
  starting transfers between devices  25.8 us (5%)
  local copies, waits for them, and re-layouts  17.3 us (4%)
  between operations  13.6 us (3%)
  matrix products  11.6 us (2%)
    all_gather x1, waiting for transfers between devices, carried_in(): gathered = lax.all_gather(x.astype(jnp.bfloat16), axis)  208 us
    all_to_all x1, blocking collectives, per_device(): lax.all_to_all(buffer, 'seq', split_axis=0, concat_axis=1, tiled=True)  177 us
    all_to_all x1, waiting for transfers between devices, per_device(): lax.all_to_all(produced_all, 'seq', split_axis=1, concat_axis=0, tiled=True)  30.5 us
    all_to_all x1, starting transfers between devices, per_device(): lax.all_to_all(jnp.stack([out_weight] * lax.axis_size('seq')), 'seq', 0, 0)  18.5 us
  transfers between devices with their start and end apart: 3, of which 2 were waited for; matrix products, arithmetic and copies ran while one was open for 2% of the time, Pallas kernels for 0%

profile of v1, /device:TPU:2, one launch (start us, length us, event | category | flops | bytes accessed | tf_op | source)
XLA Modules:
  0.0 486.6 jit_solution(1595529695661910814)
XLA Ops:
  6.5 1.2 copy.29
  7.8 2.0 convolution_convert_fusion.1
  9.8 3.2 stack.2
  13.1 18.5 %all-to-all-start = ((bf16[128,2048,8]{1,2,0:T(8,128)(2,1)}), bf16[128,2048,8]{1,2,0:T(8,128)(2,1)}, u32[]{:S(2)}, u32[]{:S(2)}) async-start(bf16[128,2048,8]{1,2,0:T(8,128)(2,1)} %stack.2), calls=%async_computation | async-start | bytes 8388608 | tf_op jit(solution)/shard_map/all_to_all | solution.py:63
  32.3 0.2 fusion.35
  33.1 1.7 convolution_bitcast_fusion.1
  34.8 207.7 %all-gather.3.cloned.1.call-done = bf16[2048,64,128]{2,1,0:T(8,128)(2,1)} async-done(((bf16[16,64,128]{2,1,0:T(8,128)(2,1)}), bf16[2048,64,128]{2,1,0:T(8,128)(2,1)}) %all-gather.3.cloned.1.call-update) | async-done | bytes 33554448 | tf_op jit(solution)/shard_map/all_gather | solution.py:16
  242.5 1.8 fusion.10
  244.3 4.0 multiply_reduce_fusion.1
  248.4 0.3 broadcast_in_dim.34
  248.7 1.0 reshape.161
  249.7 2.4 scatter_custom_fusion
  252.1 1.2 reshape.141
  253.3 177.4 %all_to_all.23 = bf16[128,1,4,1024]{3,2,1,0:T(4,128)(2,1)S(1)} all-to-all(bf16[128,1,4,1024]{3,2,1,0:T(4,128)(2,1)} %bitcast.89), channel_id=1, replica_groups=mesh['seq'=128,'win'=4] {'seq'}, dimensions={0} | all-to-all | bytes 2097152 | tf_op jit(solution)/shard_map/all_to_all | solution.py:88
  430.7 1.4 fusion.4
  432.1 0.7 fusion.7
  432.8 1.8 copy.39
  434.7 7.3 %all-to-all-start.2 = ((bf16[1,128,4,1024]{3,2,0,1:T(4,128)(2,1)}), bf16[1,128,4,1024]{3,2,0,1:T(4,128)(2,1)}, u32[]{:S(2)}, u32[]{:S(2)}) async-start(bf16[1,128,4,1024]{3,2,0,1:T(4,128)(2,1)} %copy.39), calls=%async_computation.2 | async-start | bytes 2097152 | tf_op jit(solution)/shard_map/all_to_all | solution.py:96
  442.1 30.5 %all-to-all-done.2 = bf16[1,128,4,1024]{3,2,0,1:T(4,128)(2,1)} async-done(((bf16[1,128,4,1024]{3,2,0,1:T(4,128)(2,1)}), bf16[1,128,4,1024]{3,2,0,1:T(4,128)(2,1)}, u32[]{:S(2)}, u32[]{:S(2)}) %all-to-all-start.2) | async-done | bytes 1048608 | tf_op jit(solution)/shard_map/all_to_all | solution.py:96
  472.6 1.3 reshape.146
  474.0 2.0 gather_fusion
  475.9 1.7 reshape.148
  477.6 1.3 multiply_reduce_fusion
  479.0 0.8 add_convert_fusion
  (37 shorter events, 1.5 us)
Async XLA Ops:
  6.5 424.2 %copy-start = (bf16[1,1024,768]{2,1,0:T(8,128)(2,1)S(1)}, bf16[1,1024,768]{2,1,0:T(8,128)(2,1)}, u32[]{:S(2)}) copy-start(bf16[1,1024,768]{2,1,0:T(8,128)(2,1)} %param.16) | copy-start | bytes 4718596
  6.5 235.9 %all-gather.3.cloned.1.call-start = ((), (), s32[]{:S(2)}) async-start(), calls=%async_computation.3 | async-start | bytes 33816576 | tf_op jit(solution)/shard_map/all_gather | solution.py:16
  13.1 18.5 %copy-start.2 = (s32[128,2]{0,1:T(2,128)S(1)}, s32[128,2]{0,1:T(2,128)}, u32[]{:S(2)}) copy-start(s32[128,2]{0,1:T(2,128)} %param.18) | copy-start | bytes 3076
  13.1 19.6 %copy-start.1 = (bf16[128,1024]{1,0:T(8,128)(2,1)S(1)}, bf16[128,1024]{1,0:T(8,128)(2,1)}, u32[]{:S(2)}) copy-start(bf16[128,1024]{1,0:T(8,128)(2,1)} %param.11) | copy-start | bytes 786436
  13.1 231.3 %all-to-all-start = ((bf16[128,2048,8]{1,2,0:T(8,128)(2,1)}), bf16[128,2048,8]{1,2,0:T(8,128)(2,1)}, u32[]{:S(2)}, u32[]{:S(2)}) async-start(bf16[128,2048,8]{1,2,0:T(8,128)(2,1)} %stack.2), calls=%async_computation | async-start | bytes 8388608 | tf_op jit(solution)/shard_map/all_to_all | solution.py:63
  430.7 1.4 copy-start.4
  432.8 9.2 %copy-start.3 = (f32[128,2]{0,1:T(2,128)S(1)}, f32[128,2]{0,1:T(2,128)}, u32[]{:S(2)}) copy-start(f32[128,2]{0,1:T(2,128)} %param.19) | copy-start | bytes 3076
  434.7 38.0 %all-to-all-start.2 = ((bf16[1,128,4,1024]{3,2,0,1:T(4,128)(2,1)}), bf16[1,128,4,1024]{3,2,0,1:T(4,128)(2,1)}, u32[]{:S(2)}, u32[]{:S(2)}) async-start(bf16[1,128,4,1024]{3,2,0,1:T(4,128)(2,1)} %copy.39), calls=%async_computation.2 | async-start | bytes 2097152 | tf_op jit(solution)/shard_map/all_to_all | solution.py:96
Sparse Core Ops, SparseCore 0:
  10.5 231.9 all-gather.2
